TPU v7x, 128 devices: a whole 4x4x4 slice. The times are simulated.
128 devices in a mesh: row: 8 (over x, y_lo), col: 16 (over y_hi, z, core).
Axes of the slice: x: 4, y: 4 (y_hi: 2, y_lo: 2; y = y_hi * 2 + y_lo), z: 4, core: 2. Of those that a mesh axis runs over, the one named last changes fastest.
Arguments:
- features: bfloat16 [128, 2048, 128], P('row', 'col'), may hold values from -6 to 6
- cotangent: bfloat16 [128, 2048, 128], P('row', 'col'), may hold values from -6 to 6
- w_in: bfloat16 [128, 256], replicated, may hold values from -0.5 to 0.5
- grid_in: bfloat16 [128, 256], replicated, may hold values from -0.5 to 0.5
- grid_mix: bfloat16 [256, 256], replicated, may hold values from -0.375 to 0.375
- grid_out: bfloat16 [128, 128], replicated, may hold values from -0.5 to 0.5
- block_in: bfloat16 [128, 256], replicated, may hold values from -0.5 to 0.5
- block_mix: bfloat16 [256, 256], replicated, may hold values from -0.375 to 0.375
- block_out: bfloat16 [128, 128], replicated, may hold values from -0.5 to 0.5
- w_out: bfloat16 [256, 128], replicated, may hold values from -0.375 to 0.375
Outputs:
- result: bfloat16 [128, 2048, 128], P('row', 'col')
- feature_grad: bfloat16 [128, 2048, 128], P('row', 'col')
- grad_w_in: float32 [128, 256], replicated
- grad_grid_in: float32 [128, 256], replicated
- grad_grid_mix: float32 [256, 256], replicated
- grad_grid_out: float32 [128, 128], replicated
- grad_block_in: float32 [128, 256], replicated
- grad_block_mix: float32 [256, 256], replicated
- grad_block_out: float32 [128, 128], replicated
- grad_w_out: float32 [256, 128], replicated
All inputs are finite; a program needn't handle non-finite values.
Results may differ from a plain program's by a relative error of at most 0.012.
Values may be sent and summed in bfloat16 or wider, within the bound.
A program may use at most 128 MiB of HBM per device.

v0:
```python
import math

import jax
import jax.numpy as jnp
from jax import lax
from jax.experimental import pallas as pl
from jax.experimental.pallas import tpu as pltpu
from jax.sharding import PartitionSpec as P

MESH = pl.DeviceIdType.MESH
F32 = jnp.float32
BF = jnp.bfloat16

ROWS, COLS, CH = 8, 16, 128
DEVS = ROWS * COLS
TILES = 8
TILE = 256
EARLY_A = 72
EARLY = 104
LATE = 40
LATE_AT = DEVS - LATE

epsilon = 1e-06
tanh_scale = 0.7978845608028654
cubic = 0.044715


def dot(left, right):
    return jnp.dot(left, right, preferred_element_type=F32)


def dot_nt(left, right):
    return lax.dot_general(left, right, (((1,), (1,)), ((), ())), preferred_element_type=F32)


def dot_tn(left, right):
    return lax.dot_general(left, right, (((0,), (0,)), ((), ())), preferred_element_type=F32)


def gelu_both(hidden):
    square = hidden * hidden
    inner = jnp.tanh(hidden * (tanh_scale + (tanh_scale * cubic) * square))
    half = 0.5 + 0.5 * inner
    value = hidden * half
    slope = half + value * (1.0 - half) * (2.0 * tanh_scale + (6.0 * tanh_scale * cubic) * square)
    return value, slope


def to_slots(values):
    pieces = []
    for group in range(16):
        pieces.append(values[group * 8 : group * 8 + 8])
        pieces.append(values[128 + group * 8 : 128 + group * 8 + 8])
    return jnp.concatenate(pieces, axis=0)


def from_slots(values):
    pieces = [values[group * 16 : group * 16 + 8] for group in range(16)]
    pieces += [values[group * 16 + 8 : group * 16 + 16] for group in range(16)]
    return jnp.concatenate(pieces, axis=0)


def kernel(
    feat, cot, w_in, grid_in, grid_mix, grid_out, block_in, block_mix, block_out, w_out,
    result, feature_grad, o_w_in, o_grid_in, o_grid_mix, o_grid_out, o_block_in, o_block_mix,
    o_block_out, o_w_out,
    sent, there, turned, back, x_mat, d_mat, x_mixed, d_mixed_back,
    n1_s, r1_s, slope1_s, z_s, n2_s, r2_s, slope2_s, gate_s, mix_s, mix_r_s, d_gated_s, up_s,
    joined_s, d_first_s,
    mean_mat, perm, perm_t, w_in_c, grid_in_c, block_in_c, grid_mix_t, block_mix_t,
    a_grid_in, a_grid_out, a_block_in, a_block_mix, a_block_out, a_w_in, a_w_out,
    early_out, early_in, early_all, late_out, late_in, late_all,
    send_sem, there_sem, back_sem, early_sem, early_all_sem, late_sem, late_all_sem,
):
    factor = 1.0 / math.sqrt(DEVS * TILES * TILE)
    r = lax.axis_index("row")
    c = lax.axis_index("col")
    me = r * COLS + c
    pair = c // 2
    my_slot = pair * 16 + r * 2 + lax.rem(c, 2)

    def peer_of(step):
        row = lax.rem(r + step // COLS, ROWS)
        col = lax.rem(c + lax.rem(step, COLS), COLS)
        return row, col

    barrier = pltpu.get_barrier_semaphore()

    def greet(step, carry):
        pl.semaphore_signal(barrier, inc=1, device_id=peer_of(step), device_id_type=MESH)
        return carry

    lax.fori_loop(1, DEVS, greet, 0)

    mean_mat[...] = jnp.full((CH, CH), 1.0 / CH, BF)

    def row_mean(values):
        return dot(values.astype(BF), mean_mat[...])

    def normalize(values_bf):
        values = values_bf.astype(F32)
        center = values - dot(values_bf, mean_mat[...])
        spread = lax.rsqrt(row_mean(center * center) + epsilon)
        return center * spread, spread

    def tile_of(ref, tile):
        at = pl.multiple_of(tile * 16, 16)
        return ref[:, pl.ds(at, 16), :].reshape(TILE, CH)

    def branch_pre(z_bf, upstream, in_weight, out_weight):
        unit, spread = normalize(z_bf)
        normed = unit.astype(BF)
        hidden = dot(normed, in_weight[...])
        gate, slope_gate = gelu_both(hidden[:, :CH])
        value, slope_mix = gelu_both(hidden[:, CH:])
        center = value - jnp.mean(value, axis=-1, keepdims=True)
        mix_spread = lax.rsqrt(row_mean(center * center) + epsilon)
        mix_input = center * mix_spread
        d_gated = dot_nt(upstream, out_weight[...])
        d_mixed = d_gated * gate
        return normed, spread, gate, slope_gate, slope_mix, mix_spread, mix_input, d_gated, d_mixed

    def branch_post(
        mixed, d_mix, z_bf, normed, spread, gate, slope_gate, slope_mix, mix_spread, mix_in,
        d_gated, upstream, in_centered, out_weight, acc_in, acc_out,
    ):
        mixed_one = mixed + 1.0
        gated = (gate * mixed_one).astype(BF)
        outcome = (z_bf.astype(F32) + dot(gated, out_weight[...])).astype(BF)
        acc_out[...] += dot_tn(gated, upstream)
        mix_unit = mix_in.astype(F32)
        d_value = mix_spread * (
            d_mix - row_mean(d_mix) - mix_unit * row_mean(d_mix * mix_unit)
        )
        d_hidden = jnp.concatenate(
            [(d_gated * mixed_one * slope_gate).astype(BF), (d_value * slope_mix).astype(BF)],
            axis=1,
        )
        acc_in[...] += dot_tn(normed, d_hidden)
        g = dot_nt(d_hidden, in_centered[...])
        unit = normed.astype(F32)
        d_branch = upstream.astype(F32) + spread * (g - unit * row_mean(g * unit))
        return outcome, d_branch

    def pre(step):
        tile = lax.rem(pair + step, TILES)
        x_bf = tile_of(feat, tile)
        unit, spread = normalize(x_bf)
        n1 = unit.astype(BF)
        n1_s[tile] = n1
        r1_s[tile] = spread
        value, slope = gelu_both(dot(n1, w_in[:, :CH]))
        slope1_s[tile] = slope
        z_bf = value.astype(BF)
        z_s[tile] = z_bf
        upstream = dot_nt(tile_of(cot, tile), w_out[:CH, :]).astype(BF)
        up_s[tile] = upstream
        normed, spread2, gate, slope_gate, slope_mix, mix_spread, mix_input, d_gated, d_mixed = (
            branch_pre(z_bf, upstream, grid_in, grid_out)
        )
        n2_s[tile] = normed
        r2_s[tile] = spread2
        gate_s[tile] = gate
        slope2_s[tile, :, :CH] = slope_gate
        slope2_s[tile, :, CH:] = slope_mix
        mix_r_s[tile] = mix_spread
        mix_s[tile] = mix_input.astype(BF)
        d_gated_s[tile] = d_gated
        slots = pl.ds(tile * 16, 16)
        sent[slots, 0:16, :] = to_slots(mix_input).astype(BF).reshape(16, 16, CH)
        sent[slots, 16:32, :] = to_slots(d_mixed).astype(BF).reshape(16, 16, CH)

    def send_there(step, first):
        tile = lax.rem(pair + step, TILES)

        def one(index, carry):
            row = lax.rem(r + index // 2, ROWS)
            side = lax.rem(c + index, 2)
            pltpu.make_async_remote_copy(
                src_ref=sent.at[tile * 16 + row * 2 + side],
                dst_ref=there.at[me],
                send_sem=send_sem.at[0],
                recv_sem=there_sem,
                device_id=(row, tile * 2 + side),
                device_id_type=MESH,
            ).start()
            return carry

        lax.fori_loop(first, 16, one, 0)

    pre(0)
    pl.semaphore_wait(barrier, DEVS - 1)
    pltpu.make_async_copy(sent.at[my_slot], there.at[me], there_sem).start()
    send_there(0, 1)

    def pre_step(step, carry):
        pre(step)
        send_there(step, 0)
        return carry

    lax.fori_loop(1, TILES, pre_step, 0)

    for ref, out in ((w_in, w_in_c), (grid_in, grid_in_c), (block_in, block_in_c)):
        weight = ref[...].astype(F32)
        out[...] = (weight - jnp.mean(weight, axis=0, keepdims=True)).astype(BF)
    at_row = lax.broadcasted_iota(jnp.int32, (TILE, TILE), 0)
    at_col = lax.broadcasted_iota(jnp.int32, (TILE, TILE), 1)
    eye = jnp.where(at_row == at_col, 1.0, 0.0).astype(BF)
    grid_mix_t[...] = dot_nt(eye, grid_mix[...]).astype(BF)
    block_mix_t[...] = dot_nt(eye, block_mix[...]).astype(BF)

    def place(index):
        return (index & 15) * 16 + ((index >> 4) & 1) * 8 + (index >> 5)

    perm[...] = jnp.where(at_col == place(at_row), 1.0, 0.0).astype(BF)
    perm_t[...] = jnp.where(at_row == place(at_col), 1.0, 0.0).astype(BF)
    for ref in (a_grid_in, a_grid_out, a_block_in, a_block_mix, a_block_out, a_w_in, a_w_out):
        ref[...] = jnp.zeros_like(ref)

    def block_step(tile, carry):
        n1 = n1_s[tile]
        cot_bf = tile_of(cot, tile)
        value, slope1 = gelu_both(dot(n1, w_in[:, CH:]))
        z_bf = value.astype(BF)
        upstream = dot_nt(cot_bf, w_out[CH:, :]).astype(BF)
        normed, spread, gate, slope_gate, slope_mix, mix_spread, mix_input, d_gated, d_mixed = (
            branch_pre(z_bf, upstream, block_in, block_out)
        )
        mix_in = mix_input.astype(BF)
        d_mixed = d_mixed.astype(BF)
        mixed = dot(block_mix[...], mix_in)
        d_mix = dot(block_mix_t[...], d_mixed)
        a_block_mix[...] += dot_nt(d_mixed, mix_in)
        outcome, d_branch = branch_post(
            mixed, d_mix, z_bf, normed, spread, gate, slope_gate, slope_mix, mix_spread, mix_in,
            d_gated, upstream, block_in_c, block_out, a_block_in, a_block_out,
        )
        joined_s[tile, :, CH:] = outcome
        a_w_out[CH:, :] += dot_tn(outcome, cot_bf)
        d_first = (d_branch * slope1).astype(BF)
        d_first_s[tile, :, CH:] = d_first
        a_w_in[:, CH:] += dot_tn(n1, d_first)
        return carry

    lax.fori_loop(0, TILES, block_step, 0)

    def pack(out, at, values):
        for left in range(0, values.shape[1], CH):
            count = values.shape[0] // 16
            piece = values[:, left : left + CH] * factor
            out[at : at + count] = piece.astype(BF).reshape(count, 16, CH)
            at += count
        return at

    def unpack(src, at, shape):
        halves = []
        for _ in range(0, shape[1], CH):
            count = shape[0] // 16
            halves.append(src[at : at + count].reshape(shape[0], CH).astype(F32))
            at += count
        return jnp.concatenate(halves, axis=1) if len(halves) > 1 else halves[0]

    at = pack(early_out, 0, a_block_in[...])
    at = pack(early_out, at, a_block_mix[...])
    at = pack(early_out, at, a_block_out[...])
    at = pack(early_out, at, a_w_out[CH:, :])
    pack(early_out, at, a_w_in[:, CH:])

    def scatter(out, into, least, most, shift, send, recv):
        def one(step, carry):
            row, col = peer_of(step)
            chunk = row * COLS + col - shift

            @pl.when((chunk >= least) & (chunk < most))
            def _():
                pltpu.make_async_remote_copy(
                    src_ref=out.at[chunk],
                    dst_ref=into.at[me],
                    send_sem=send,
                    recv_sem=recv,
                    device_id=(row, col),
                    device_id_type=MESH,
                ).start()

            return carry

        lax.fori_loop(1, DEVS, one, 0)

    def gather(buffer, chunk, send, recv):
        def one(step, carry):
            pltpu.make_async_remote_copy(
                src_ref=buffer.at[chunk],
                dst_ref=buffer.at[chunk],
                send_sem=send,
                recv_sem=recv,
                device_id=peer_of(step),
                device_id_type=MESH,
            ).start()
            return carry

        lax.fori_loop(1, DEVS, one, 0)

    def wait_for(sem, buffer, count):
        pltpu.make_async_copy(
            buffer.at[pl.ds(0, count)], buffer.at[pl.ds(0, count)], sem
        ).wait()

    scatter(early_out, early_in, 0, EARLY_A, 0, send_sem.at[2], early_sem)

    wait_for(there_sem, there, DEVS)

    def gather_positions(row, carry):
        source = pl.ds(row * 16, 16)
        at = pl.ds(pl.multiple_of(row * 32, 32), 32)
        for part, out in ((0, x_mat), (16, d_mat)):
            values = there[source, part : part + 16, :].reshape(TILE, CH)
            values = dot(perm[...], values).astype(BF)
            for offset in range(8):
                out[at, offset * CH : (offset + 1) * CH] = values[offset * 32 : offset * 32 + 32]
        return carry

    lax.fori_loop(0, ROWS, gather_positions, 0)
    x_mixed[...] = dot(grid_mix[...], x_mat[...]).astype(BF)
    d_mixed_back[...] = dot(grid_mix_t[...], d_mat[...]).astype(BF)

    def scatter_positions(row, carry):
        target = pl.ds(row * 16, 16)
        at = pl.ds(pl.multiple_of(row * 32, 32), 32)
        for part, src in ((0, x_mixed), (16, d_mixed_back)):
            values = jnp.concatenate(
                [src[at, offset * CH : (offset + 1) * CH] for offset in range(8)], axis=0
            )
            turned[target, part : part + 16, :] = (
                dot(perm_t[...], values).astype(BF).reshape(16, 16, CH)
            )
        return carry

    lax.fori_loop(0, ROWS, scatter_positions, 0)

    pltpu.make_async_copy(turned.at[me], back.at[my_slot], back_sem.at[pair]).start()

    def send_back(index, carry):
        tile = lax.rem(pair + index // 16, TILES)
        row = lax.rem(r + lax.rem(index, 16) // 2, ROWS)
        side = lax.rem(c + index, 2)
        col = tile * 2 + side
        pltpu.make_async_remote_copy(
            src_ref=turned.at[row * COLS + col],
            dst_ref=back.at[my_slot],
            send_sem=send_sem.at[1],
            recv_sem=back_sem.at[pair],
            device_id=(row, col),
            device_id_type=MESH,
        ).start()
        return carry

    lax.fori_loop(1, DEVS, send_back, 0)

    pack(early_out, EARLY_A, dot_nt(d_mat[...], x_mat[...]))
    scatter(early_out, early_in, EARLY_A, EARLY, 0, send_sem.at[2], early_sem)

    def reduce_chunk(out, into, every, chunk, send, recv, recv_all):
        into[me] = out[chunk]
        wait_for(recv, into, DEVS - 1)

        def add(index, total):
            return total + jnp.sum(into[pl.ds(index * 16, 16)].astype(F32), axis=0)

        total = lax.fori_loop(0, DEVS // 16, add, jnp.zeros((16, CH), F32))
        every[chunk] = total.astype(BF)
        gather(every, chunk, send, recv_all)

    @pl.when(me < EARLY)
    def _():
        reduce_chunk(
            early_out, early_in, early_all, me, send_sem.at[3], early_sem, early_all_sem
        )

    def grid_step(step, carry):
        tile = lax.rem(pair + TILES - step, TILES)
        wait_for(back_sem.at[tile], back, 16)
        slots = pl.ds(tile * 16, 16)
        mixed = from_slots(back[slots, 0:16, :].reshape(TILE, CH).astype(F32))
        d_mix = from_slots(back[slots, 16:32, :].reshape(TILE, CH).astype(F32))
        x_bf = tile_of(feat, tile)
        cot_bf = tile_of(cot, tile)
        n1 = n1_s[tile]
        outcome, d_branch = branch_post(
            mixed, d_mix, z_s[tile], n2_s[tile], r2_s[tile], gate_s[tile],
            slope2_s[tile, :, :CH], slope2_s[tile, :, CH:], mix_r_s[tile], mix_s[tile],
            d_gated_s[tile], up_s[tile], grid_in_c, grid_out, a_grid_in, a_grid_out,
        )
        joined = jnp.concatenate([outcome, joined_s[tile, :, CH:]], axis=1)
        a_w_out[:CH, :] += dot_tn(outcome, cot_bf)
        d_first = (d_branch * slope1_s[tile]).astype(BF)
        a_w_in[:, :CH] += dot_tn(n1, d_first)
        d_both = jnp.concatenate([d_first, d_first_s[tile, :, CH:]], axis=1)
        at = pl.ds(pl.multiple_of(tile * 16, 16), 16)
        out = (x_bf.astype(F32) + dot(joined, w_out[...])).astype(BF)
        result[:, at, :] = out.reshape(16, 16, CH)
        g = dot_nt(d_both, w_in_c[...])
        unit = n1.astype(F32)
        grad = cot_bf.astype(F32) + r1_s[tile] * (g - unit * row_mean(g * unit))
        feature_grad[:, at, :] = grad.astype(BF).reshape(16, 16, CH)
        return carry

    lax.fori_loop(0, TILES, grid_step, 0)

    at = pack(late_out, 0, a_grid_in[...])
    at = pack(late_out, at, a_grid_out[...])
    at = pack(late_out, at, a_w_out[:CH, :])
    pack(late_out, at, a_w_in[:, :CH])
    scatter(late_out, late_in, 0, LATE, LATE_AT, send_sem.at[4], late_sem)

    @pl.when(me >= LATE_AT)
    def _():
        reduce_chunk(
            late_out, late_in, late_all, me - LATE_AT, send_sem.at[5], late_sem, late_all_sem
        )

    @pl.when(me < EARLY)
    def _():
        wait_for(early_all_sem, early_all, EARLY - 1)
        wait_for(send_sem.at[2], early_out, EARLY - 1)

    @pl.when(me >= EARLY)
    def _():
        wait_for(early_all_sem, early_all, EARLY)
        wait_for(send_sem.at[2], early_out, EARLY)

    o_block_in[...] = unpack(early_all, 0, (128, 256))
    o_block_mix[...] = unpack(early_all, 16, (256, 256))
    o_block_out[...] = unpack(early_all, 48, (128, 128))
    o_w_out[CH:, :] = unpack(early_all, 56, (128, 128))
    o_w_in[:, CH:] = unpack(early_all, 64, (128, 128))
    o_grid_mix[...] = unpack(early_all, 72, (256, 256))

    wait_for(send_sem.at[0], sent, DEVS - 1)
    wait_for(send_sem.at[1], turned, DEVS - 1)

    @pl.when(me < EARLY)
    def _():
        wait_for(send_sem.at[3], early_in, DEVS - 1)

    @pl.when(me < LATE_AT)
    def _():
        wait_for(late_all_sem, late_all, LATE)
        wait_for(send_sem.at[4], late_out, LATE)

    @pl.when(me >= LATE_AT)
    def _():
        wait_for(late_all_sem, late_all, LATE - 1)
        wait_for(send_sem.at[4], late_out, LATE - 1)
        wait_for(send_sem.at[5], late_in, DEVS - 1)

    o_grid_in[...] = unpack(late_all, 0, (128, 256))
    o_grid_out[...] = unpack(late_all, 16, (128, 128))
    o_w_out[:CH, :] = unpack(late_all, 24, (128, 128))
    o_w_in[:, :CH] = unpack(late_all, 32, (128, 128))


def body(*args):
    def whole(dtype, *shape):
        return pltpu.VMEM(shape, dtype)

    pixels = (TILES, TILE, CH)
    both = (TILES, TILE, 2 * CH)
    scratch = [
        *[whole(BF, DEVS, 32, CH)] * 4,
        *[whole(BF, 256, 8 * CH)] * 4,
        whole(BF, *pixels),
        whole(F32, *pixels),
        whole(F32, *pixels),
        whole(BF, *pixels),
        whole(BF, *pixels),
        whole(F32, *pixels),
        whole(F32, *both),
        whole(F32, *pixels),
        whole(BF, *pixels),
        whole(F32, *pixels),
        whole(F32, *pixels),
        whole(BF, *pixels),
        whole(BF, *both),
        whole(BF, *both),
        whole(BF, CH, CH),
        *[whole(BF, TILE, TILE)] * 2,
        *[whole(BF, CH, 2 * CH)] * 3,
        *[whole(BF, 256, 256)] * 2,
        whole(F32, CH, 2 * CH),
        whole(F32, CH, CH),
        whole(F32, CH, 2 * CH),
        whole(F32, 256, 256),
        whole(F32, CH, CH),
        whole(F32, CH, 2 * CH),
        whole(F32, 2 * CH, CH),
        whole(BF, EARLY, 16, CH),
        whole(BF, DEVS, 16, CH),
        whole(BF, EARLY, 16, CH),
        whole(BF, LATE, 16, CH),
        whole(BF, DEVS, 16, CH),
        whole(BF, LATE, 16, CH),
        pltpu.SemaphoreType.DMA((6,)),
        pltpu.SemaphoreType.DMA,
        pltpu.SemaphoreType.DMA((TILES,)),
        *[pltpu.SemaphoreType.DMA] * 4,
    ]
    vmem = pl.BlockSpec(memory_space=pltpu.VMEM)
    shape = args[0].shape
    outs = [
        jax.ShapeDtypeStruct(shape, BF),
        jax.ShapeDtypeStruct(shape, BF),
        jax.ShapeDtypeStruct((128, 256), F32),
        jax.ShapeDtypeStruct((128, 256), F32),
        jax.ShapeDtypeStruct((256, 256), F32),
        jax.ShapeDtypeStruct((128, 128), F32),
        jax.ShapeDtypeStruct((128, 256), F32),
        jax.ShapeDtypeStruct((256, 256), F32),
        jax.ShapeDtypeStruct((128, 128), F32),
        jax.ShapeDtypeStruct((256, 128), F32),
    ]
    return tuple(
        pl.pallas_call(
            kernel,
            out_shape=outs,
            in_specs=[vmem] * 10,
            out_specs=[vmem] * 10,
            scratch_shapes=scratch,
            compiler_params=pltpu.CompilerParams(
                collective_id=0, has_side_effects=True, vmem_limit_bytes=56 * 2**20
            ),
        )(*args)
    )


def solution(mesh):
    split = P("row", "col", None)
    return jax.shard_map(
        body,
        mesh=mesh,
        in_specs=(split, split) + (P(),) * 8,
        out_specs=(split, split) + (P(),) * 8,
        check_vma=False,
    )
```

profile of v0, /device:TPU:1, one launch (start us, length us, event | category | flops | bytes accessed | tf_op | source)
XLA Modules:
  0.0 111.0 jit_solution(12822800373191674944)
XLA Ops:
  0.6 101.4 %shard_map.177 = (bf16[16,128,128]{2,1,0:T(8,128)(2,1)}, bf16[16,128,128]{2,1,0:T(8,128)(2,1)}, f32[128,256]{1,0:T(8,128)}, f32[128,256]{1,0:T(8,128)}, f32[256,...) custom-call(bf16[16,128,128]{2,1,0:T(8,128)(2,1)} %feat.1, ...), custom_call_target="tpu_custom_call" | custom-call | tf_op jit(solution)/shard_map/pallas_call | solution.py:522
  102.1 0.0 copy-start
  102.1 1.9 %copy.30 = bf16[16,128,128]{2,1,0:T(8,128)(2,1)} copy(bf16[16,128,128]{2,1,0:T(8,128)(2,1)} %get-tuple-element.20) | data formatting | bytes 1048576
  104.0 0.0 copy-done
  104.0 0.0 copy-start.6
  104.0 0.0 copy-start.5
  104.0 0.8 copy.31
  104.8 0.2 copy-done.6
  105.0 0.0 copy-start.2
  105.0 0.7 copy.32
  105.7 0.0 copy-done.5
  105.7 0.7 copy.33
  106.4 0.0 copy-done.2
  106.4 0.7 copy.34
  107.1 0.2 copy-done.8
  107.2 0.6 copy.35
  107.9 0.0 copy-done.4
  107.9 0.7 copy.36
  108.5 0.0 copy-done.1
  108.5 0.7 copy.37
  109.2 0.2 copy-done.7
  109.4 0.6 copy.38
  110.0 0.3 copy-done.3
  110.3 0.7 copy.39
  (5 shorter events, 0.0 us)
Async XLA Ops:
  102.1 2.0 %copy-start = (bf16[16,128,128]{2,1,0:T(8,128)(2,1)S(1)}, bf16[16,128,128]{2,1,0:T(8,128)(2,1)}, u32[]{:S(2)}) copy-start(bf16[16,128,128]{2,1,0:T(8,128)(2,1)} %get-tuple-element.21) | copy-start | bytes 1572868
  104.0 1.0 copy-start.6
  104.0 1.7 %copy-start.5 = (f32[128,256]{1,0:T(8,128)S(1)}, f32[128,256]{1,0:T(8,128)}, u32[]{:S(2)}) copy-start(f32[128,256]{1,0:T(8,128)} %get-tuple-element.23) | copy-start | bytes 393220
  105.0 1.3 %copy-start.2 = (f32[256,256]{1,0:T(8,128)S(1)}, f32[256,256]{1,0:T(8,128)}, u32[]{:S(2)}) copy-start(f32[256,256]{1,0:T(8,128)} %get-tuple-element.24) | copy-start | bytes 786436
  106.4 0.9 copy-start.8
  106.4 1.5 %copy-start.4 = (f32[128,256]{1,0:T(8,128)S(1)}, f32[128,256]{1,0:T(8,128)}, u32[]{:S(2)}) copy-start(f32[128,256]{1,0:T(8,128)} %get-tuple-element.26) | copy-start | bytes 393220
  107.2 1.3 %copy-start.1 = (f32[256,256]{1,0:T(8,128)S(1)}, f32[256,256]{1,0:T(8,128)}, u32[]{:S(2)}) copy-start(f32[256,256]{1,0:T(8,128)} %get-tuple-element.27) | copy-start | bytes 786436
  108.5 0.9 copy-start.7
  109.4 0.9 copy-start.3
where the time goes:
time: 111 us
  Pallas kernels  101 us (91%)
  local copies, waits for them, and re-layouts  8.86 us (8%)
    pallas_call x1, Pallas kernels, body(): pl.pallas_call(kernel, out_shape=outs, in_specs=[vmem] * 10, out_specs=[v...  101 us
    unnamed x28, local copies, waits for them, and re-layouts  8.86 us

commit v1 on v0

--- a/solution.py
+++ b/solution.py
@@ -18,7 +18,9 @@
 EARLY_A = 72
 EARLY = 104
 LATE = 40
-LATE_AT = DEVS - LATE
+SPREAD = 3
+UNSPREAD = 43
+PRE_FIRST = 4
 
 epsilon = 1e-06
 tanh_scale = 0.7978845608028654
@@ -61,21 +63,22 @@
 
 
 def kernel(
-    feat, cot, w_in, grid_in, grid_mix, grid_out, block_in, block_mix, block_out, w_out,
-    result, feature_grad, o_w_in, o_grid_in, o_grid_mix, o_grid_out, o_block_in, o_block_mix,
-    o_block_out, o_w_out,
-    sent, there, turned, back, x_mat, d_mat, x_mixed, d_mixed_back,
+    feat_hbm, cot_hbm, w_in, grid_in, grid_mix, grid_out, block_in, block_mix, block_out, w_out,
+    result, feature_grad, early_res, late_res,
+    feat, cot, result_v, feature_grad_v, sent, there, turned, back, x_mat, d_mat, x_mixed, d_mixed_back,
     n1_s, r1_s, slope1_s, z_s, n2_s, r2_s, slope2_s, gate_s, mix_s, mix_r_s, d_gated_s, up_s,
     joined_s, d_first_s,
-    mean_mat, perm, perm_t, w_in_c, grid_in_c, block_in_c, grid_mix_t, block_mix_t,
+    perm, perm_t, w_in_ct, grid_in_ct, block_in_ct, grid_mix_t, block_mix_t, w_out_t, grid_out_t,
+    block_out_t,
     a_grid_in, a_grid_out, a_block_in, a_block_mix, a_block_out, a_w_in, a_w_out,
     early_out, early_in, early_all, late_out, late_in, late_all,
-    send_sem, there_sem, back_sem, early_sem, early_all_sem, late_sem, late_all_sem,
+    send_sem, there_sem, back_sem, early_sem, early_all_sem, late_sem, late_all_sem, io_sem,
 ):
     factor = 1.0 / math.sqrt(DEVS * TILES * TILE)
     r = lax.axis_index("row")
     c = lax.axis_index("col")
     me = r * COLS + c
+    mine = lax.rem(me * UNSPREAD, DEVS)
     pair = c // 2
     my_slot = pair * 16 + r * 2 + lax.rem(c, 2)
 
@@ -84,6 +87,11 @@
         col = lax.rem(c + lax.rem(step, COLS), COLS)
         return row, col
 
+    feat_in = pltpu.make_async_copy(feat_hbm, feat, io_sem.at[0])
+    cot_in = pltpu.make_async_copy(cot_hbm, cot, io_sem.at[1])
+    feat_in.start()
+    cot_in.start()
+
     barrier = pltpu.get_barrier_semaphore()
 
     def greet(step, carry):
@@ -92,14 +100,12 @@
 
     lax.fori_loop(1, DEVS, greet, 0)
 
-    mean_mat[...] = jnp.full((CH, CH), 1.0 / CH, BF)
-
     def row_mean(values):
-        return dot(values.astype(BF), mean_mat[...])
+        return jnp.mean(values, axis=-1, keepdims=True)
 
     def normalize(values_bf):
         values = values_bf.astype(F32)
-        center = values - dot(values_bf, mean_mat[...])
+        center = values - row_mean(values)
         spread = lax.rsqrt(row_mean(center * center) + epsilon)
         return center * spread, spread
 
@@ -107,22 +113,22 @@
         at = pl.multiple_of(tile * 16, 16)
         return ref[:, pl.ds(at, 16), :].reshape(TILE, CH)
 
-    def branch_pre(z_bf, upstream, in_weight, out_weight):
+    def branch_pre(z_bf, upstream, in_weight, out_weight_t):
         unit, spread = normalize(z_bf)
         normed = unit.astype(BF)
         hidden = dot(normed, in_weight[...])
         gate, slope_gate = gelu_both(hidden[:, :CH])
         value, slope_mix = gelu_both(hidden[:, CH:])
-        center = value - jnp.mean(value, axis=-1, keepdims=True)
+        center = value - row_mean(value)
         mix_spread = lax.rsqrt(row_mean(center * center) + epsilon)
         mix_input = center * mix_spread
-        d_gated = dot_nt(upstream, out_weight[...])
+        d_gated = dot(upstream, out_weight_t[...])
         d_mixed = d_gated * gate
         return normed, spread, gate, slope_gate, slope_mix, mix_spread, mix_input, d_gated, d_mixed
 
     def branch_post(
         mixed, d_mix, z_bf, normed, spread, gate, slope_gate, slope_mix, mix_spread, mix_in,
-        d_gated, upstream, in_centered, out_weight, acc_in, acc_out,
+        d_gated, upstream, in_centered_t, out_weight, acc_in, acc_out,
     ):
         mixed_one = mixed + 1.0
         gated = (gate * mixed_one).astype(BF)
@@ -137,7 +143,7 @@
             axis=1,
         )
         acc_in[...] += dot_tn(normed, d_hidden)
-        g = dot_nt(d_hidden, in_centered[...])
+        g = dot(d_hidden, in_centered_t[...])
         unit = normed.astype(F32)
         d_branch = upstream.astype(F32) + spread * (g - unit * row_mean(g * unit))
         return outcome, d_branch
@@ -148,22 +154,22 @@
         unit, spread = normalize(x_bf)
         n1 = unit.astype(BF)
         n1_s[tile] = n1
-        r1_s[tile] = spread
+        r1_s[tile] = jnp.broadcast_to(spread, (TILE, CH))
         value, slope = gelu_both(dot(n1, w_in[:, :CH]))
         slope1_s[tile] = slope
         z_bf = value.astype(BF)
         z_s[tile] = z_bf
-        upstream = dot_nt(tile_of(cot, tile), w_out[:CH, :]).astype(BF)
+        upstream = dot(tile_of(cot, tile), w_out_t[:, :CH]).astype(BF)
         up_s[tile] = upstream
         normed, spread2, gate, slope_gate, slope_mix, mix_spread, mix_input, d_gated, d_mixed = (
-            branch_pre(z_bf, upstream, grid_in, grid_out)
+            branch_pre(z_bf, upstream, grid_in, grid_out_t)
         )
         n2_s[tile] = normed
-        r2_s[tile] = spread2
+        r2_s[tile] = jnp.broadcast_to(spread2, (TILE, CH))
         gate_s[tile] = gate
         slope2_s[tile, :, :CH] = slope_gate
         slope2_s[tile, :, CH:] = slope_mix
-        mix_r_s[tile] = mix_spread
+        mix_r_s[tile] = jnp.broadcast_to(mix_spread, (TILE, CH))
         mix_s[tile] = mix_input.astype(BF)
         d_gated_s[tile] = d_gated
         slots = pl.ds(tile * 16, 16)
@@ -188,43 +194,54 @@
 
         lax.fori_loop(first, 16, one, 0)
 
-    pre(0)
+    at_row = lax.broadcasted_iota(jnp.int32, (TILE, TILE), 0)
+    at_col = lax.broadcasted_iota(jnp.int32, (TILE, TILE), 1)
+    eye = jnp.where(at_row == at_col, 1.0, 0.0).astype(BF)
+    eye_half = eye[:CH, :CH]
+    w_out_t[...] = dot_nt(eye_half, w_out[...]).astype(BF)
+    grid_out_t[...] = dot_nt(eye_half, grid_out[...]).astype(BF)
+
+    def prepare():
+        block_out_t[...] = dot_nt(eye_half, block_out[...]).astype(BF)
+        for ref, out in ((w_in, w_in_ct), (grid_in, grid_in_ct), (block_in, block_in_ct)):
+            weight = ref[...].astype(F32)
+            centered = (weight - jnp.mean(weight, axis=0, keepdims=True)).astype(BF)
+            out[...] = dot_nt(eye, centered).astype(BF)
+        grid_mix_t[...] = dot_nt(eye, grid_mix[...]).astype(BF)
+        block_mix_t[...] = dot_nt(eye, block_mix[...]).astype(BF)
+
+        def place(index):
+            return (index & 15) * 16 + ((index >> 4) & 1) * 8 + (index >> 5)
+
+        perm[...] = jnp.where(at_col == place(at_row), 1.0, 0.0).astype(BF)
+        perm_t[...] = jnp.where(at_row == place(at_col), 1.0, 0.0).astype(BF)
+        for ref in (a_grid_in, a_grid_out, a_block_in, a_block_mix, a_block_out, a_w_in, a_w_out):
+            ref[...] = jnp.zeros_like(ref)
+
+    feat_in.wait()
+    cot_in.wait()
+    prepare()
+    lax.fori_loop(0, PRE_FIRST, lambda step, carry: (pre(step), carry)[1], 0)
     pl.semaphore_wait(barrier, DEVS - 1)
     pltpu.make_async_copy(sent.at[my_slot], there.at[me], there_sem).start()
     send_there(0, 1)
+    lax.fori_loop(1, PRE_FIRST, lambda step, carry: (send_there(step, 0), carry)[1], 0)
 
     def pre_step(step, carry):
         pre(step)
         send_there(step, 0)
         return carry
 
-    lax.fori_loop(1, TILES, pre_step, 0)
-
-    for ref, out in ((w_in, w_in_c), (grid_in, grid_in_c), (block_in, block_in_c)):
-        weight = ref[...].astype(F32)
-        out[...] = (weight - jnp.mean(weight, axis=0, keepdims=True)).astype(BF)
-    at_row = lax.broadcasted_iota(jnp.int32, (TILE, TILE), 0)
-    at_col = lax.broadcasted_iota(jnp.int32, (TILE, TILE), 1)
-    eye = jnp.where(at_row == at_col, 1.0, 0.0).astype(BF)
-    grid_mix_t[...] = dot_nt(eye, grid_mix[...]).astype(BF)
-    block_mix_t[...] = dot_nt(eye, block_mix[...]).astype(BF)
-
-    def place(index):
-        return (index & 15) * 16 + ((index >> 4) & 1) * 8 + (index >> 5)
-
-    perm[...] = jnp.where(at_col == place(at_row), 1.0, 0.0).astype(BF)
-    perm_t[...] = jnp.where(at_row == place(at_col), 1.0, 0.0).astype(BF)
-    for ref in (a_grid_in, a_grid_out, a_block_in, a_block_mix, a_block_out, a_w_in, a_w_out):
-        ref[...] = jnp.zeros_like(ref)
+    lax.fori_loop(PRE_FIRST, TILES, pre_step, 0)
 
     def block_step(tile, carry):
         n1 = n1_s[tile]
         cot_bf = tile_of(cot, tile)
         value, slope1 = gelu_both(dot(n1, w_in[:, CH:]))
         z_bf = value.astype(BF)
-        upstream = dot_nt(cot_bf, w_out[CH:, :]).astype(BF)
+        upstream = dot(cot_bf, w_out_t[:, CH:]).astype(BF)
         normed, spread, gate, slope_gate, slope_mix, mix_spread, mix_input, d_gated, d_mixed = (
-            branch_pre(z_bf, upstream, block_in, block_out)
+            branch_pre(z_bf, upstream, block_in, block_out_t)
         )
         mix_in = mix_input.astype(BF)
         d_mixed = d_mixed.astype(BF)
@@ -233,7 +250,7 @@
         a_block_mix[...] += dot_nt(d_mixed, mix_in)
         outcome, d_branch = branch_post(
             mixed, d_mix, z_bf, normed, spread, gate, slope_gate, slope_mix, mix_spread, mix_in,
-            d_gated, upstream, block_in_c, block_out, a_block_in, a_block_out,
+            d_gated, upstream, block_in_ct, block_out, a_block_in, a_block_out,
         )
         joined_s[tile, :, CH:] = outcome
         a_w_out[CH:, :] += dot_tn(outcome, cot_bf)
@@ -242,7 +259,12 @@
         a_w_in[:, CH:] += dot_tn(n1, d_first)
         return carry
 
-    lax.fori_loop(0, TILES, block_step, 0)
+    def block_pair(index, carry):
+        block_step(index * 2, 0)
+        block_step(index * 2 + 1, 0)
+        return carry
+
+    lax.fori_loop(0, TILES // 2, block_pair, 0)
 
     def pack(out, at, values):
         for left in range(0, values.shape[1], CH):
@@ -252,39 +274,25 @@
             at += count
         return at
 
-    def unpack(src, at, shape):
-        halves = []
-        for _ in range(0, shape[1], CH):
-            count = shape[0] // 16
-            halves.append(src[at : at + count].reshape(shape[0], CH).astype(F32))
-            at += count
-        return jnp.concatenate(halves, axis=1) if len(halves) > 1 else halves[0]
-
-    at = pack(early_out, 0, a_block_in[...])
-    at = pack(early_out, at, a_block_mix[...])
-    at = pack(early_out, at, a_block_out[...])
-    at = pack(early_out, at, a_w_out[CH:, :])
-    pack(early_out, at, a_w_in[:, CH:])
-
-    def scatter(out, into, least, most, shift, send, recv):
-        def one(step, carry):
-            row, col = peer_of(step)
-            chunk = row * COLS + col - shift
-
-            @pl.when((chunk >= least) & (chunk < most))
+    def scatter(out, into, least, most, send, recv):
+        def one(index, carry):
+            chunk = least + lax.rem(index + me, most - least)
+            to = lax.rem(chunk * SPREAD, DEVS)
+
+            @pl.when(to != me)
             def _():
                 pltpu.make_async_remote_copy(
                     src_ref=out.at[chunk],
                     dst_ref=into.at[me],
                     send_sem=send,
                     recv_sem=recv,
-                    device_id=(row, col),
+                    device_id=(to // COLS, lax.rem(to, COLS)),
                     device_id_type=MESH,
                 ).start()
 
             return carry
 
-        lax.fori_loop(1, DEVS, one, 0)
+        lax.fori_loop(0, most - least, one, 0)
 
     def gather(buffer, chunk, send, recv):
         def one(step, carry):
@@ -305,7 +313,12 @@
             buffer.at[pl.ds(0, count)], buffer.at[pl.ds(0, count)], sem
         ).wait()
 
-    scatter(early_out, early_in, 0, EARLY_A, 0, send_sem.at[2], early_sem)
+    at = pack(early_out, 0, a_block_in[...])
+    at = pack(early_out, at, a_block_mix[...])
+    at = pack(early_out, at, a_block_out[...])
+    at = pack(early_out, at, a_w_out[CH:, :])
+    pack(early_out, at, a_w_in[:, CH:])
+    scatter(early_out, early_in, 0, EARLY_A, send_sem.at[2], early_sem)
 
     wait_for(there_sem, there, DEVS)
 
@@ -320,6 +333,8 @@
         return carry
 
     lax.fori_loop(0, ROWS, gather_positions, 0)
+    pack(early_out, EARLY_A, dot_nt(d_mat[...], x_mat[...]))
+    scatter(early_out, early_in, EARLY_A, EARLY, send_sem.at[2], early_sem)
     x_mixed[...] = dot(grid_mix[...], x_mat[...]).astype(BF)
     d_mixed_back[...] = dot(grid_mix_t[...], d_mat[...]).astype(BF)
 
@@ -356,9 +371,6 @@
 
     lax.fori_loop(1, DEVS, send_back, 0)
 
-    pack(early_out, EARLY_A, dot_nt(d_mat[...], x_mat[...]))
-    scatter(early_out, early_in, EARLY_A, EARLY, 0, send_sem.at[2], early_sem)
-
     def reduce_chunk(out, into, every, chunk, send, recv, recv_all):
         into[me] = out[chunk]
         wait_for(recv, into, DEVS - 1)
@@ -370,10 +382,10 @@
         every[chunk] = total.astype(BF)
         gather(every, chunk, send, recv_all)
 
-    @pl.when(me < EARLY)
+    @pl.when(mine < EARLY)
     def _():
         reduce_chunk(
-            early_out, early_in, early_all, me, send_sem.at[3], early_sem, early_all_sem
+            early_out, early_in, early_all, mine, send_sem.at[3], early_sem, early_all_sem
         )
 
     def grid_step(step, carry):
@@ -388,7 +400,7 @@
         outcome, d_branch = branch_post(
             mixed, d_mix, z_s[tile], n2_s[tile], r2_s[tile], gate_s[tile],
             slope2_s[tile, :, :CH], slope2_s[tile, :, CH:], mix_r_s[tile], mix_s[tile],
-            d_gated_s[tile], up_s[tile], grid_in_c, grid_out, a_grid_in, a_grid_out,
+            d_gated_s[tile], up_s[tile], grid_in_ct, grid_out, a_grid_in, a_grid_out,
         )
         joined = jnp.concatenate([outcome, joined_s[tile, :, CH:]], axis=1)
         a_w_out[:CH, :] += dot_tn(outcome, cot_bf)
@@ -397,66 +409,97 @@
         d_both = jnp.concatenate([d_first, d_first_s[tile, :, CH:]], axis=1)
         at = pl.ds(pl.multiple_of(tile * 16, 16), 16)
         out = (x_bf.astype(F32) + dot(joined, w_out[...])).astype(BF)
-        result[:, at, :] = out.reshape(16, 16, CH)
-        g = dot_nt(d_both, w_in_c[...])
+        result_v[:, at, :] = out.reshape(16, 16, CH)
+        g = dot(d_both, w_in_ct[...])
         unit = n1.astype(F32)
         grad = cot_bf.astype(F32) + r1_s[tile] * (g - unit * row_mean(g * unit))
-        feature_grad[:, at, :] = grad.astype(BF).reshape(16, 16, CH)
+        feature_grad_v[:, at, :] = grad.astype(BF).reshape(16, 16, CH)
         return carry
 
     lax.fori_loop(0, TILES, grid_step, 0)
+    result_out = pltpu.make_async_copy(result_v, result, io_sem.at[2])
+    feature_grad_out = pltpu.make_async_copy(feature_grad_v, feature_grad, io_sem.at[3])
+    result_out.start()
+    feature_grad_out.start()
 
     at = pack(late_out, 0, a_grid_in[...])
     at = pack(late_out, at, a_grid_out[...])
     at = pack(late_out, at, a_w_out[:CH, :])
     pack(late_out, at, a_w_in[:, :CH])
-    scatter(late_out, late_in, 0, LATE, LATE_AT, send_sem.at[4], late_sem)
-
-    @pl.when(me >= LATE_AT)
+    scatter(late_out, late_in, 0, LATE, send_sem.at[4], late_sem)
+
+    @pl.when(mine < LATE)
     def _():
         reduce_chunk(
-            late_out, late_in, late_all, me - LATE_AT, send_sem.at[5], late_sem, late_all_sem
-        )
-
-    @pl.when(me < EARLY)
+            late_out, late_in, late_all, mine, send_sem.at[5], late_sem, late_all_sem
+        )
+
+    @pl.when(mine < EARLY)
     def _():
         wait_for(early_all_sem, early_all, EARLY - 1)
         wait_for(send_sem.at[2], early_out, EARLY - 1)
 
-    @pl.when(me >= EARLY)
+    @pl.when(mine >= EARLY)
     def _():
         wait_for(early_all_sem, early_all, EARLY)
         wait_for(send_sem.at[2], early_out, EARLY)
 
+    wait_for(send_sem.at[0], sent, DEVS - 1)
+    wait_for(send_sem.at[1], turned, DEVS - 1)
+
+    @pl.when(mine < EARLY)
+    def _():
+        wait_for(send_sem.at[3], early_in, DEVS - 1)
+
+    @pl.when(mine >= LATE)
+    def _():
+        wait_for(late_all_sem, late_all, LATE)
+        wait_for(send_sem.at[4], late_out, LATE)
+
+    @pl.when(mine < LATE)
+    def _():
+        wait_for(late_all_sem, late_all, LATE - 1)
+        wait_for(send_sem.at[4], late_out, LATE - 1)
+        wait_for(send_sem.at[5], late_in, DEVS - 1)
+
+    early_res[...] = early_all[...]
+    late_res[...] = late_all[...]
+    result_out.wait()
+    feature_grad_out.wait()
+
+
+def unpack(src, at, shape):
+    halves = []
+    for _ in range(0, shape[1], CH):
+        count = shape[0] // 16
+        halves.append(src[at : at + count].reshape(shape[0], CH).astype(F32))
+        at += count
+    return jnp.concatenate(halves, axis=1) if len(halves) > 1 else halves[0]
+
+
+def finish(
+    result_in, feature_grad_in, early_all, late_all,
+    result, feature_grad, o_w_in, o_grid_in, o_grid_mix, o_grid_out, o_block_in, o_block_mix,
+    o_block_out, o_w_out, sem,
+):
+    copies = [
+        pltpu.make_async_copy(result_in, result, sem.at[0]),
+        pltpu.make_async_copy(feature_grad_in, feature_grad, sem.at[1]),
+    ]
+    for copy in copies:
+        copy.start()
     o_block_in[...] = unpack(early_all, 0, (128, 256))
     o_block_mix[...] = unpack(early_all, 16, (256, 256))
     o_block_out[...] = unpack(early_all, 48, (128, 128))
     o_w_out[CH:, :] = unpack(early_all, 56, (128, 128))
     o_w_in[:, CH:] = unpack(early_all, 64, (128, 128))
     o_grid_mix[...] = unpack(early_all, 72, (256, 256))
-
-    wait_for(send_sem.at[0], sent, DEVS - 1)
-    wait_for(send_sem.at[1], turned, DEVS - 1)
-
-    @pl.when(me < EARLY)
-    def _():
-        wait_for(send_sem.at[3], early_in, DEVS - 1)
-
-    @pl.when(me < LATE_AT)
-    def _():
-        wait_for(late_all_sem, late_all, LATE)
-        wait_for(send_sem.at[4], late_out, LATE)
-
-    @pl.when(me >= LATE_AT)
-    def _():
-        wait_for(late_all_sem, late_all, LATE - 1)
-        wait_for(send_sem.at[4], late_out, LATE - 1)
-        wait_for(send_sem.at[5], late_in, DEVS - 1)
-
     o_grid_in[...] = unpack(late_all, 0, (128, 256))
     o_grid_out[...] = unpack(late_all, 16, (128, 128))
     o_w_out[:CH, :] = unpack(late_all, 24, (128, 128))
     o_w_in[:, :CH] = unpack(late_all, 32, (128, 128))
+    for copy in copies:
+        copy.wait()
 
 
 def body(*args):
@@ -466,6 +509,7 @@
     pixels = (TILES, TILE, CH)
     both = (TILES, TILE, 2 * CH)
     scratch = [
+        *[whole(BF, 16, 128, CH)] * 4,
         *[whole(BF, DEVS, 32, CH)] * 4,
         *[whole(BF, 256, 8 * CH)] * 4,
         whole(BF, *pixels),
@@ -482,10 +526,11 @@
         whole(BF, *pixels),
         whole(BF, *both),
         whole(BF, *both),
-        whole(BF, CH, CH),
         *[whole(BF, TILE, TILE)] * 2,
-        *[whole(BF, CH, 2 * CH)] * 3,
+        *[whole(BF, 2 * CH, CH)] * 3,
         *[whole(BF, 256, 256)] * 2,
+        whole(BF, CH, 2 * CH),
+        *[whole(BF, CH, CH)] * 2,
         whole(F32, CH, 2 * CH),
         whole(F32, CH, CH),
         whole(F32, CH, 2 * CH),
@@ -503,6 +548,7 @@
         pltpu.SemaphoreType.DMA,
         pltpu.SemaphoreType.DMA((TILES,)),
         *[pltpu.SemaphoreType.DMA] * 4,
+        pltpu.SemaphoreType.DMA((4,)),
     ]
     vmem = pl.BlockSpec(memory_space=pltpu.VMEM)
     shape = args[0].shape
@@ -518,17 +564,30 @@
         jax.ShapeDtypeStruct((128, 128), F32),
         jax.ShapeDtypeStruct((256, 128), F32),
     ]
+    hbm = pl.BlockSpec(memory_space=pl.ANY)
+    parts = pl.pallas_call(
+        kernel,
+        out_shape=[
+            outs[0],
+            outs[1],
+            jax.ShapeDtypeStruct((EARLY, 16, CH), BF),
+            jax.ShapeDtypeStruct((LATE, 16, CH), BF),
+        ],
+        in_specs=[hbm] * 2 + [vmem] * 8,
+        out_specs=[hbm] * 2 + [vmem] * 2,
+        scratch_shapes=scratch,
+        compiler_params=pltpu.CompilerParams(
+            collective_id=0, has_side_effects=True, vmem_limit_bytes=56 * 2**20
+        ),
+    )(*args)
     return tuple(
         pl.pallas_call(
-            kernel,
+            finish,
             out_shape=outs,
-            in_specs=[vmem] * 10,
-            out_specs=[vmem] * 10,
-            scratch_shapes=scratch,
-            compiler_params=pltpu.CompilerParams(
-                collective_id=0, has_side_effects=True, vmem_limit_bytes=56 * 2**20
-            ),
-        )(*args)
+            in_specs=[vmem] * 4,
+            out_specs=[hbm] * 2 + [vmem] * 8,
+            scratch_shapes=[pltpu.SemaphoreType.DMA((2,))],
+        )(*parts)
     )
 
 

time: 111 us -> 81.1 us (0.73)
  Pallas kernels: 101 us -> 80.3 us
  local copies, waits for them, and re-layouts: 8.86 us -> 0 us
    pallas_call x1 -> x2, Pallas kernels: 101 us -> 80.3 us  [the longest x1 77 us: body(): pl.pallas_call(kernel, out_shape=[outs[0], outs[1], jax.ShapeDtypeStruct(...]
    unnamed x28 -> x0, local copies, waits for them, and re-layouts: 8.86 us -> none
where the time goes in v1:
time: 81.1 us; the launch traced here: 81 us
  Pallas kernels  80.3 us (99%)
    pallas_call x1, Pallas kernels, body(): pl.pallas_call(kernel, out_shape=[outs[0], outs[1], jax.ShapeDtypeStruct(...  77 us
    pallas_call x1, Pallas kernels, body(): pl.pallas_call(finish, out_shape=outs, in_specs=[vmem] * 4, out_specs=[hb...  3.35 us

profile of v1, /device:TPU:1, one launch (start us, length us, event | category | flops | bytes accessed | tf_op | source)
XLA Modules:
  0.0 81.0 jit_solution(13512758554827861048)
XLA Ops:
  0.6 77.0 %shard_map.177 = (bf16[16,128,128]{2,1,0:T(8,128)(2,1)}, bf16[16,128,128]{2,1,0:T(8,128)(2,1)}, bf16[104,16,128]{2,1,0:T(8,128)(2,1)}, bf16[40,16,128]{2,1,0:T(8,128)(2,1)}) custom-call(bf16[16,128,128]{2,1,0:T(8,128)(2,1)} %feat_hbm.1, bf16[16,128,128]{2,1,0:T(8,128)(2,1)} %cot_hbm.1, bf16[128,256]{1,0:T(8,128)(2,1)} %w_in.1, bf16[128,256]{1,0:T(8,128)(2,1)} %grid_in.1, ...), custom_call_target="tpu_custom_call" | custom-call | tf_op jit(solution)/shard_map/pallas_call | solution.py:568
  77.6 3.3 %shard_map.178 = (bf16[16,128,128]{2,1,0:T(8,128)(2,1)}, bf16[16,128,128]{2,1,0:T(8,128)(2,1)}, f32[128,256]{1,0:T(8,128)}, f32[128,256]{1,0:T(8,128)}, f32[256,...) custom-call(bf16[16,128,128]{2,1,0:T(8,128)(2,1)} %get-tuple-element, ...), custom_call_target="tpu_custom_call" | custom-call | tf_op jit(solution)/shard_map/pallas_call | solution.py:584

commit v2 on v1

--- a/solution.py
+++ b/solution.py
@@ -332,7 +332,7 @@
                 out[at, offset * CH : (offset + 1) * CH] = values[offset * 32 : offset * 32 + 32]
         return carry
 
-    lax.fori_loop(0, ROWS, gather_positions, 0)
+    lax.fori_loop(0, ROWS, gather_positions, 0, unroll=True)
     pack(early_out, EARLY_A, dot_nt(d_mat[...], x_mat[...]))
     scatter(early_out, early_in, EARLY_A, EARLY, send_sem.at[2], early_sem)
     x_mixed[...] = dot(grid_mix[...], x_mat[...]).astype(BF)
@@ -350,7 +350,7 @@
             )
         return carry
 
-    lax.fori_loop(0, ROWS, scatter_positions, 0)
+    lax.fori_loop(0, ROWS, scatter_positions, 0, unroll=True)
 
     pltpu.make_async_copy(turned.at[me], back.at[my_slot], back_sem.at[pair]).start()
 
@@ -382,19 +382,12 @@
         every[chunk] = total.astype(BF)
         gather(every, chunk, send, recv_all)
 
-    @pl.when(mine < EARLY)
-    def _():
-        reduce_chunk(
-            early_out, early_in, early_all, mine, send_sem.at[3], early_sem, early_all_sem
-        )
-
     def grid_step(step, carry):
         tile = lax.rem(pair + TILES - step, TILES)
         wait_for(back_sem.at[tile], back, 16)
         slots = pl.ds(tile * 16, 16)
         mixed = from_slots(back[slots, 0:16, :].reshape(TILE, CH).astype(F32))
         d_mix = from_slots(back[slots, 16:32, :].reshape(TILE, CH).astype(F32))
-        x_bf = tile_of(feat, tile)
         cot_bf = tile_of(cot, tile)
         n1 = n1_s[tile]
         outcome, d_branch = branch_post(
@@ -402,31 +395,54 @@
             slope2_s[tile, :, :CH], slope2_s[tile, :, CH:], mix_r_s[tile], mix_s[tile],
             d_gated_s[tile], up_s[tile], grid_in_ct, grid_out, a_grid_in, a_grid_out,
         )
-        joined = jnp.concatenate([outcome, joined_s[tile, :, CH:]], axis=1)
+        joined_s[tile, :, :CH] = outcome
         a_w_out[:CH, :] += dot_tn(outcome, cot_bf)
         d_first = (d_branch * slope1_s[tile]).astype(BF)
         a_w_in[:, :CH] += dot_tn(n1, d_first)
-        d_both = jnp.concatenate([d_first, d_first_s[tile, :, CH:]], axis=1)
+        d_first_s[tile, :, :CH] = d_first
+        return carry
+
+    def output_step(tile, carry):
+        x_bf = tile_of(feat, tile)
+        cot_bf = tile_of(cot, tile)
+        n1 = n1_s[tile]
         at = pl.ds(pl.multiple_of(tile * 16, 16), 16)
-        out = (x_bf.astype(F32) + dot(joined, w_out[...])).astype(BF)
+        out = (x_bf.astype(F32) + dot(joined_s[tile], w_out[...])).astype(BF)
         result_v[:, at, :] = out.reshape(16, 16, CH)
-        g = dot(d_both, w_in_ct[...])
+        g = dot(d_first_s[tile], w_in_ct[...])
         unit = n1.astype(F32)
         grad = cot_bf.astype(F32) + r1_s[tile] * (g - unit * row_mean(g * unit))
         feature_grad_v[:, at, :] = grad.astype(BF).reshape(16, 16, CH)
         return carry
 
-    lax.fori_loop(0, TILES, grid_step, 0)
-    result_out = pltpu.make_async_copy(result_v, result, io_sem.at[2])
-    feature_grad_out = pltpu.make_async_copy(feature_grad_v, feature_grad, io_sem.at[3])
-    result_out.start()
-    feature_grad_out.start()
-
+    def output_pair(index, carry):
+        output_step(index * 2, 0)
+        output_step(index * 2 + 1, 0)
+        return carry
+
+    def grid_pair(index, carry):
+        grid_step(index * 2, 0)
+        grid_step(index * 2 + 1, 0)
+        return carry
+
+    lax.fori_loop(0, TILES // 2, grid_pair, 0)
     at = pack(late_out, 0, a_grid_in[...])
     at = pack(late_out, at, a_grid_out[...])
     at = pack(late_out, at, a_w_out[:CH, :])
     pack(late_out, at, a_w_in[:, :CH])
     scatter(late_out, late_in, 0, LATE, send_sem.at[4], late_sem)
+
+    lax.fori_loop(0, TILES // 2, output_pair, 0)
+    result_out = pltpu.make_async_copy(result_v, result, io_sem.at[2])
+    feature_grad_out = pltpu.make_async_copy(feature_grad_v, feature_grad, io_sem.at[3])
+    result_out.start()
+    feature_grad_out.start()
+
+    @pl.when(mine < EARLY)
+    def _():
+        reduce_chunk(
+            early_out, early_in, early_all, mine, send_sem.at[3], early_sem, early_all_sem
+        )
 
     @pl.when(mine < LATE)
     def _():

time: 81.1 us -> 75.2 us (0.927)
  Pallas kernels: 80.3 us -> 74.4 us
    pallas_call x1, Pallas kernels: 77 us -> 71.1 us  [body(): pl.pallas_call(kernel, out_shape=[outs[0], outs[1], jax.ShapeDtypeStruct(...]
where the time goes in v2:
time: 75.2 us; the launch traced here: 75.1 us
  Pallas kernels  74.4 us (99%)
    pallas_call x1, Pallas kernels, body(): pl.pallas_call(kernel, out_shape=[outs[0], outs[1], jax.ShapeDtypeStruct(...  71.1 us
    pallas_call x1, Pallas kernels, body(): pl.pallas_call(finish, out_shape=outs, in_specs=[vmem] * 4, out_specs=[hb...  3.35 us

profile of v2, /device:TPU:1, one launch (start us, length us, event | category | flops | bytes accessed | tf_op | source)
XLA Modules:
  0.0 75.1 jit_solution(6831594117299782814)
XLA Ops:
  0.6 71.1 %shard_map.177 = (bf16[16,128,128]{2,1,0:T(8,128)(2,1)}, bf16[16,128,128]{2,1,0:T(8,128)(2,1)}, bf16[104,16,128]{2,1,0:T(8,128)(2,1)}, bf16[40,16,128]{2,1,0:T(8,128)(2,1)}) custom-call(bf16[16,128,128]{2,1,0:T(8,128)(2,1)} %feat_hbm.1, bf16[16,128,128]{2,1,0:T(8,128)(2,1)} %cot_hbm.1, bf16[128,256]{1,0:T(8,128)(2,1)} %w_in.1, bf16[128,256]{1,0:T(8,128)(2,1)} %grid_in.1, ...), custom_call_target="tpu_custom_call" | custom-call | tf_op jit(solution)/shard_map/pallas_call | solution.py:584
  71.7 3.3 %shard_map.178 = (bf16[16,128,128]{2,1,0:T(8,128)(2,1)}, bf16[16,128,128]{2,1,0:T(8,128)(2,1)}, f32[128,256]{1,0:T(8,128)}, f32[128,256]{1,0:T(8,128)}, f32[256,...) custom-call(bf16[16,128,128]{2,1,0:T(8,128)(2,1)} %get-tuple-element, ...), custom_call_target="tpu_custom_call" | custom-call | tf_op jit(solution)/shard_map/pallas_call | solution.py:600

commit v3 on v2

--- a/solution.py
+++ b/solution.py
@@ -83,8 +83,8 @@
     my_slot = pair * 16 + r * 2 + lax.rem(c, 2)
 
     def peer_of(step):
-        row = lax.rem(r + step // COLS, ROWS)
-        col = lax.rem(c + lax.rem(step, COLS), COLS)
+        row = lax.rem(r + lax.rem(step, ROWS), ROWS)
+        col = lax.rem(c + step // ROWS, COLS)
         return row, col
 
     feat_in = pltpu.make_async_copy(feat_hbm, feat, io_sem.at[0])
@@ -180,8 +180,8 @@
         tile = lax.rem(pair + step, TILES)
 
         def one(index, carry):
-            row = lax.rem(r + index // 2, ROWS)
-            side = lax.rem(c + index, 2)
+            row = lax.rem(r + index, ROWS)
+            side = lax.rem(c + index // ROWS, 2)
             pltpu.make_async_remote_copy(
                 src_ref=sent.at[tile * 16 + row * 2 + side],
                 dst_ref=there.at[me],
@@ -356,8 +356,8 @@
 
     def send_back(index, carry):
         tile = lax.rem(pair + index // 16, TILES)
-        row = lax.rem(r + lax.rem(index, 16) // 2, ROWS)
-        side = lax.rem(c + index, 2)
+        row = lax.rem(r + index, ROWS)
+        side = lax.rem(c + index // ROWS, 2)
         col = tile * 2 + side
         pltpu.make_async_remote_copy(
             src_ref=turned.at[row * COLS + col],
@@ -378,7 +378,7 @@
         def add(index, total):
             return total + jnp.sum(into[pl.ds(index * 16, 16)].astype(F32), axis=0)
 
-        total = lax.fori_loop(0, DEVS // 16, add, jnp.zeros((16, CH), F32))
+        total = lax.fori_loop(0, DEVS // 16, add, jnp.zeros((16, CH), F32), unroll=True)
         every[chunk] = total.astype(BF)
         gather(every, chunk, send, recv_all)
 
@@ -494,16 +494,27 @@
 
 
 def finish(
-    result_in, feature_grad_in, early_all, late_all,
+    result_in, feature_grad_in, early_in, late_in,
     result, feature_grad, o_w_in, o_grid_in, o_grid_mix, o_grid_out, o_block_in, o_block_mix,
-    o_block_out, o_w_out, sem,
+    o_block_out, o_w_out, result_v, feature_grad_v, early_all, late_all, sem,
 ):
+    arrivals = [
+        pltpu.make_async_copy(result_in, result_v, sem.at[0]),
+        pltpu.make_async_copy(feature_grad_in, feature_grad_v, sem.at[1]),
+        pltpu.make_async_copy(early_in, early_all, sem.at[2]),
+        pltpu.make_async_copy(late_in, late_all, sem.at[3]),
+    ]
     copies = [
-        pltpu.make_async_copy(result_in, result, sem.at[0]),
-        pltpu.make_async_copy(feature_grad_in, feature_grad, sem.at[1]),
+        pltpu.make_async_copy(result_v, result, sem.at[4]),
+        pltpu.make_async_copy(feature_grad_v, feature_grad, sem.at[5]),
     ]
-    for copy in copies:
+    for arrival in arrivals:
+        arrival.start()
+    for arrival, copy in zip(arrivals, copies):
+        arrival.wait()
         copy.start()
+    arrivals[2].wait()
+    arrivals[3].wait()
     o_block_in[...] = unpack(early_all, 0, (128, 256))
     o_block_mix[...] = unpack(early_all, 16, (256, 256))
     o_block_out[...] = unpack(early_all, 48, (128, 128))
@@ -600,9 +611,15 @@
         pl.pallas_call(
             finish,
             out_shape=outs,
-            in_specs=[vmem] * 4,
+            in_specs=[hbm] * 4,
             out_specs=[hbm] * 2 + [vmem] * 8,
-            scratch_shapes=[pltpu.SemaphoreType.DMA((2,))],
+            scratch_shapes=[
+                pltpu.VMEM(shape, BF),
+                pltpu.VMEM(shape, BF),
+                pltpu.VMEM(parts[2].shape, BF),
+                pltpu.VMEM(parts[3].shape, BF),
+                pltpu.SemaphoreType.DMA((6,)),
+            ],
         )(*parts)
     )
 

time: 75.2 us -> 74.2 us (0.987)
  Pallas kernels: 74.4 us -> 73.3 us
    pallas_call x1, Pallas kernels: 71.1 us -> 70.3 us  [body(): pl.pallas_call(kernel, out_shape=[outs[0], outs[1], jax.ShapeDtypeStruct(...]
where the time goes in v3:
time: 74.2 us; the launch traced here: 74 us
  Pallas kernels  73.3 us (99%)
    pallas_call x1, Pallas kernels, body(): pl.pallas_call(kernel, out_shape=[outs[0], outs[1], jax.ShapeDtypeStruct(...  70.3 us
    pallas_call x1, Pallas kernels, body(): pl.pallas_call(finish, out_shape=outs, in_specs=[hbm] * 4, out_specs=[hbm...  3.06 us

profile of v3, /device:TPU:1, one launch (start us, length us, event | category | flops | bytes accessed | tf_op | source)
XLA Modules:
  0.0 74.0 jit_solution(4431288512032194789)
XLA Ops:
  0.6 70.3 %shard_map.177 = (bf16[16,128,128]{2,1,0:T(8,128)(2,1)}, bf16[16,128,128]{2,1,0:T(8,128)(2,1)}, bf16[104,16,128]{2,1,0:T(8,128)(2,1)}, bf16[40,16,128]{2,1,0:T(8,128)(2,1)}) custom-call(bf16[16,128,128]{2,1,0:T(8,128)(2,1)} %feat_hbm.1, bf16[16,128,128]{2,1,0:T(8,128)(2,1)} %cot_hbm.1, bf16[128,256]{1,0:T(8,128)(2,1)} %w_in.1, bf16[128,256]{1,0:T(8,128)(2,1)} %grid_in.1, ...), custom_call_target="tpu_custom_call" | custom-call | tf_op jit(solution)/shard_map/pallas_call | solution.py:595
  70.9 3.1 %shard_map.178 = (bf16[16,128,128]{2,1,0:T(8,128)(2,1)}, bf16[16,128,128]{2,1,0:T(8,128)(2,1)}, f32[128,256]{1,0:T(8,128)}, f32[128,256]{1,0:T(8,128)}, f32[256,...) custom-call(bf16[16,128,128]{2,1,0:T(8,128)(2,1)} %get-tuple-element, ...), custom_call_target="tpu_custom_call" | custom-call | tf_op jit(solution)/shard_map/pallas_call | solution.py:611

commit v4 on v3

--- a/solution.py
+++ b/solution.py
@@ -98,7 +98,7 @@
         pl.semaphore_signal(barrier, inc=1, device_id=peer_of(step), device_id_type=MESH)
         return carry
 
-    lax.fori_loop(1, DEVS, greet, 0)
+    lax.fori_loop(1, DEVS, greet, 0, unroll=8)
 
     def row_mean(values):
         return jnp.mean(values, axis=-1, keepdims=True)
@@ -306,7 +306,7 @@
             ).start()
             return carry
 
-        lax.fori_loop(1, DEVS, one, 0)
+        lax.fori_loop(1, DEVS, one, 0, unroll=8)
 
     def wait_for(sem, buffer, count):
         pltpu.make_async_copy(
@@ -460,6 +460,8 @@
         wait_for(early_all_sem, early_all, EARLY)
         wait_for(send_sem.at[2], early_out, EARLY)
 
+    early_copy = pltpu.make_async_copy(early_all, early_res, io_sem.at[0])
+    early_copy.start()
     wait_for(send_sem.at[0], sent, DEVS - 1)
     wait_for(send_sem.at[1], turned, DEVS - 1)
 
@@ -478,8 +480,10 @@
         wait_for(send_sem.at[4], late_out, LATE - 1)
         wait_for(send_sem.at[5], late_in, DEVS - 1)
 
-    early_res[...] = early_all[...]
-    late_res[...] = late_all[...]
+    late_copy = pltpu.make_async_copy(late_all, late_res, io_sem.at[1])
+    late_copy.start()
+    early_copy.wait()
+    late_copy.wait()
     result_out.wait()
     feature_grad_out.wait()
 
@@ -601,7 +605,7 @@
             jax.ShapeDtypeStruct((LATE, 16, CH), BF),
         ],
         in_specs=[hbm] * 2 + [vmem] * 8,
-        out_specs=[hbm] * 2 + [vmem] * 2,
+        out_specs=[hbm] * 4,
         scratch_shapes=scratch,
         compiler_params=pltpu.CompilerParams(
             collective_id=0, has_side_effects=True, vmem_limit_bytes=56 * 2**20

time: 74.2 us -> 74.2 us (level)
  no operation moved by 1% of the time
where the time goes in v4:
time: 74.2 us; the launch traced here: 74 us
  Pallas kernels  73.4 us (99%)
    pallas_call x1, Pallas kernels, body(): pl.pallas_call(kernel, out_shape=[outs[0], outs[1], jax.ShapeDtypeStruct(...  70.3 us
    pallas_call x1, Pallas kernels, body(): pl.pallas_call(finish, out_shape=outs, in_specs=[hbm] * 4, out_specs=[hbm...  3.06 us

profile of v4, /device:TPU:1, one launch (start us, length us, event | category | flops | bytes accessed | tf_op | source)
XLA Modules:
  0.0 74.0 jit_solution(16955239826344128622)
XLA Ops:
  0.6 70.3 %shard_map.177 = (bf16[16,128,128]{2,1,0:T(8,128)(2,1)}, bf16[16,128,128]{2,1,0:T(8,128)(2,1)}, bf16[104,16,128]{2,1,0:T(8,128)(2,1)}, bf16[40,16,128]{2,1,0:T(8,128)(2,1)}) custom-call(bf16[16,128,128]{2,1,0:T(8,128)(2,1)} %feat_hbm.1, bf16[16,128,128]{2,1,0:T(8,128)(2,1)} %cot_hbm.1, bf16[128,256]{1,0:T(8,128)(2,1)} %w_in.1, bf16[128,256]{1,0:T(8,128)(2,1)} %grid_in.1, ...), custom_call_target="tpu_custom_call" | custom-call | tf_op jit(solution)/shard_map/pallas_call | solution.py:599
  70.9 3.1 %shard_map.178 = (bf16[16,128,128]{2,1,0:T(8,128)(2,1)}, bf16[16,128,128]{2,1,0:T(8,128)(2,1)}, f32[128,256]{1,0:T(8,128)}, f32[128,256]{1,0:T(8,128)}, f32[256,...) custom-call(bf16[16,128,128]{2,1,0:T(8,128)(2,1)} %get-tuple-element, ...), custom_call_target="tpu_custom_call" | custom-call | tf_op jit(solution)/shard_map/pallas_call | solution.py:615
